TPU v7x, 32 devices: a whole 2x2x4 slice. The times are simulated.
32 devices in a mesh: grp: 2 (over y), pair: 4 (over z), ga: 2 (over x), sub: 2 (over core).
Axes of the slice: x: 2, y: 2, z: 4, core: 2. Of those that a mesh axis runs over, the one named last changes fastest.
Arguments:
- densities: bfloat16 [256, 122880], P(('grp', 'pair'), 'ga'), parts along dimension 0, may hold values from -6 to 6
- eigvecs: bfloat16 [2, 61440, 2048], P('ga', 'pair', 'sub'), may hold values from -0.015625 to 0.015625
- energies: float32 [256], P('grp'), parts along dimension 0, may hold values from 0.1 to 2
- frequencies: float32 [4], replicated, may hold values from 0.05 to 2
Outputs:
- chi_sub: float32 [8, 2048, 2048], P('grp', 'sub', ('pair', 'ga')), parts along dimension 0
There are 2 independent parts, one for each index of `grp`. A program takes and returns all parts, laid end to end along the dimension named above; an argument that names none is the same for every part. Nothing has to cross between parts.
All inputs are finite; a program needn't handle non-finite values.
Results may differ from a plain program's by a relative error of at most 0.0048.
Values may be sent and summed in bfloat16 or wider, within the bound.
A program may use at most 128 MiB of HBM per device.

v0:
```python
import jax
import jax.numpy as jnp
from jax import lax
from jax.sharding import PartitionSpec as P


def from_partner(array, axis, stride):
    return lax.ppermute(array, axis, [(i, i ^ 1 << stride) for i in range(lax.axis_size(axis))])


def on_device(densities, eigvecs, energies, frequencies):
    exchanged = lax.all_to_all(densities, "pair", split_axis=1, concat_axis=0, tiled=True)
    local_basis = eigvecs[0]
    total_pairs = exchanged.shape[0]
    half_width = local_basis.shape[1]
    partial_value = jnp.dot(exchanged, local_basis, preferred_element_type=jnp.float32)
    coefficients = lax.psum(partial_value, ("pair", "ga")).astype(jnp.bfloat16)
    n_blocks = lax.axis_size("pair") * lax.axis_size("ga")
    block_width = 2 * half_width // n_blocks
    block_index = lax.axis_index("pair") * lax.axis_size("ga") + lax.axis_index("ga")
    my_half = lax.axis_index("sub")
    block_start = block_index * block_width
    other_half = from_partner(coefficients, "sub", 0)
    whole_coef = jnp.where(
        my_half == 0,
        jnp.concatenate([coefficients, other_half], axis=1),
        jnp.concatenate([other_half, coefficients], axis=1),
    )
    columns = lax.dynamic_slice_in_dim(whole_coef, block_start, block_width, 1)
    squared = energies * energies
    factor = (
        2.0 * energies[None, :] / (squared[None, :] + frequencies[:, None] * frequencies[:, None])
    )
    weighted = (factor[:, :, None] * columns.astype(jnp.float32)[None, :, :]).astype(jnp.bfloat16)
    result = jnp.einsum("ps,wpt->wst", coefficients, weighted, preferred_element_type=jnp.float32)
    return result * (-1.0 / total_pairs)


def solution(mesh):
    placed = (P(("grp", "pair"), "ga"), P("ga", "pair", "sub"), P("grp"), P())
    return jax.shard_map(
        on_device,
        mesh=mesh,
        in_specs=placed,
        out_specs=P("grp", "sub", ("pair", "ga")),
        check_vma=False,
    )
```

profile of v0, /device:TPU:0, one launch (start us, length us, event | category | flops | bytes accessed | tf_op | source)
XLA Modules:
  0.0 159.9 jit_solution(17883082448071864179)
XLA Ops:
  0.0 2.4 %copy.17 = bf16[4,4,8,15360]{3,2,0,1:T(8,128)(2,1)S(1)} copy(bf16[4,4,8,15360]{3,2,1,0:T(8,128)(2,1)} %bitcast.18) | data formatting | bytes 7864320 | tf_op jit(solution)/shard_map/all_to_all | solution.py:12
  2.4 93.6 %all_to_all.19 = bf16[32,4,15360]{2,0,1:T(8,128)(2,1)S(1)} all-to-all(bf16[32,4,15360]{2,0,1:T(8,128)(2,1)S(1)} %bitcast.17), channel_id=1, replica_groups=mesh['grp'=2,'pair'=4,'ga'=2,'sub'=2] {'pair'}, dimensions={1} | all-to-all | bytes 7864320 | tf_op jit(solution)/shard_map/all_to_all | solution.py:12
  96.0 0.0 copy-start
  96.0 0.0 copy-start.1
  96.0 12.4 %fusion = f32[128,1024]{1,0:T(8,128)S(1)} fusion(bf16[128,15360]{1,0:T(8,128)(2,1)S(1)} %bitcast.16, bf16[1,15360,1024]{2,1,0:T(8,128)(2,1)} %param.5), kind=kOutput, calls=%fused_computation | convolution fusion | flops 4026531840 | bytes 35913728 | tf_op jit(solution)/shard_map/dot_general | solution.py:16
  108.5 41.6 %all-reduce.1 = bf16[128,1024]{1,0:T(8,128)(2,1)S(1)} all-reduce(f32[128,1024]{1,0:T(8,128)S(1)} %fusion), channel_id=1, replica_groups=mesh['grp'=2,'pair'=4,'ga'=2,'sub'=2] {'pair','ga'}, use_global_device_ids=true, to_apply=%region_0.0 | all-reduce | flops 131072 | bytes 786432 | tf_op jit(solution)/shard_map/psum | solution.py:17
  150.1 0.1 collective-permute-start
  150.2 0.0 copy-done
  150.2 0.0 copy-done.1
  150.2 0.1 add_divide_fusion
  150.3 1.4 collective-permute-done
  151.7 0.1 select_convert_fusion
  151.8 0.1 copy.13
  151.9 2.6 %multiply_bitcast_fusion = f32[4,1024,256]{1,2,0:T(8,128)} fusion(bf16[128,1024]{1,0:T(8,128)(2,1)S(1)} %all-reduce.1, f32[128,256]{0,1:T(8,128)S(1)} %copy.13, f32[4,128]{1,0:T(4,128)S(1)} %add_divide_fusion), kind=kOutput, calls=%fused_computation.2 | convolution fusion | flops 269746176 | bytes 4589568 | tf_op jit(solution)/shard_map/ps,wpt->wst/dot_general | solution.py:35
  154.5 5.4 %copy.14 = f32[4,1024,256]{2,1,0:T(8,128)} copy(f32[4,1024,256]{1,2,0:T(8,128)} %multiply_bitcast_fusion) | data formatting | bytes 8388608 | tf_op jit(solution)/shard_map/mul | solution.py:36
  (2 shorter events, 0.0 us)
Async XLA Ops:
  96.0 54.2 %copy-start = (f32[128]{0:T(128)S(1)}, f32[128]{0:T(128)}, u32[]{:S(2)}) copy-start(f32[128]{0:T(128)} %param.6) | copy-start | bytes 1540
  96.0 54.2 %copy-start.1 = (f32[4]{0:T(128)S(1)}, f32[4]{0:T(128)}, u32[]{:S(2)}) copy-start(f32[4]{0:T(128)} %param.7) | copy-start | bytes 52
  150.1 1.6 %collective-permute-start = (bf16[128,1024]{1,0:T(8,128)(2,1)S(1)}, bf16[128,1024]{1,0:T(8,128)(2,1)S(1)}, u32[]{:S(2)}, u32[]{:S(2)}) collective-permute-start(bf16[128,1024]{1,0:T(8,128)(2,1)S(1)} %all-reduce.1), channel_id=1, source_target_pairs={{0,1},{1,0},{2,3},{3,2},{4,5},{5,4},{6,7},{7,6},{8,9},{9,8},{10,11... | collective-permute-start | bytes 786440 | tf_op jit(solution)/shard_map/ppermute | solution.py:8
where the time goes:
time: 160 us
  blocking collectives  135 us (84%)
  matrix products  15.1 us (9%)
  local copies, waits for them, and re-layouts  7.83 us (5%)
    all_to_all x1, blocking collectives, on_device(): lax.all_to_all(densities, 'pair', split_axis=1, concat_axis=0, tiled=True)  93.6 us
    psum x1, blocking collectives, on_device(): coefficients = lax.psum(partial_value, ('pair', 'ga')).astype(jnp.bfloat16)  41.6 us
    dot_general x1, matrix products, on_device(): jnp.dot(exchanged, local_basis, preferred_element_type=jnp.float32)  12.4 us
    mul x1, local copies, waits for them, and re-layouts, on_device(): return result * (-1.0 / total_pairs)  5.36 us
  transfers between devices with their start and end apart: 1, of which 1 were waited for; matrix products, arithmetic and copies ran while one was open for 0% of the time, Pallas kernels for 0%

commit v1 on v0

v1 whole, which is shorter than its diff:
```python
import functools

import jax
import jax.numpy as jnp
from jax import lax
from jax.experimental import pallas as pl
from jax.experimental.pallas import tpu as pltpu
from jax.sharding import PartitionSpec as P

MESH = pl.DeviceIdType.MESH
WIDTH = 1536
TILE = 256


def flipped(index, bits):
    bit = 1
    while bit <= bits:
        if bits & bit:
            index = index + bit - 2 * bit * ((index // bit) % 2)
        bit *= 2
    return index


def span(start, size, unit):
    return pl.ds(pl.multiple_of(start, unit), size)


def kernel(n, n_ga, chunks, with_tail, dens, basis, *refs):
    if with_tail:
        (coef_out, block_out, eig, exch, total, sums, coef, other,
         eig_sem, own_sem, send, recv, fwd_send, fwd_recv,
         sum_send, sum_recv, all_send, all_recv, sib_send, sib_recv) = refs
    else:
        total, eig, exch, eig_sem, own_sem, send, recv, fwd_send, fwd_recv = refs
    z, x, c = lax.axis_index("pair"), lax.axis_index("ga"), lax.axis_index("sub")
    depth, half = eig.shape
    rows = exch.shape[1]
    part = rows // 2
    width = depth // chunks
    groups = n * n_ga
    rank = z * n_ga + x
    pieced = len(dens.shape) == 3

    def cols(k):
        return slice(None) if chunks == 1 else span(k * width, width, 128)

    def eig_copy(k):
        at = span(k * width, width, 16)
        return pltpu.make_async_copy(basis.at[0, at], eig.at[at], eig_sem.at[k])

    def own_copy():
        src = dens.at[z] if pieced else dens.at[:, span(z * depth, depth, 128)]
        return pltpu.make_async_copy(src, exch.at[z], own_sem)

    mine = span(c * part, part, part)

    def sending(k, d):
        to = flipped(z, d)
        if pieced:
            src = dens.at[to, mine]
        else:
            src = dens.at[mine, span(to * depth + k * width, width, 128)]
        return pltpu.make_async_remote_copy(
            src_ref=src, dst_ref=exch.at[z, mine, cols(k)],
            send_sem=send.at[k, d - 1], recv_sem=recv.at[k, d - 1],
            device_id={"pair": to}, device_id_type=MESH)

    def forwarding(k, d):
        here = exch.at[flipped(z, d), mine, cols(k)]
        return pltpu.make_async_remote_copy(
            src_ref=here, dst_ref=here,
            send_sem=fwd_send.at[k, d - 1], recv_sem=fwd_recv.at[k, d - 1],
            device_id={"sub": 1 - c}, device_id_type=MESH)

    def peer(e):
        to = flipped(rank, e)
        return to, {"pair": to // n_ga, "ga": to % n_ga}

    def loop(count, body):
        lax.fori_loop(0, count, lambda i, _: (body(i), 0)[1], 0)

    loop(chunks, lambda k: eig_copy(k).start())
    own_copy().start()

    barrier = pltpu.get_barrier_semaphore()
    greeted = range(1, groups) if with_tail else range(n_ga, groups, n_ga)
    for e in greeted:
        pl.semaphore_signal(barrier, inc=1, device_id=peer(e)[1], device_id_type=MESH)
    pl.semaphore_signal(barrier, inc=1, device_id={"sub": 1 - c}, device_id_type=MESH)
    pl.semaphore_wait(barrier, len(greeted) + 1)

    far_first = range(n - 1, 0, -1)

    def send_chunk(k):
        for d in far_first:
            sending(k, d).start()

    loop(chunks, send_chunk)
    total[...] = jnp.zeros_like(total)
    own_copy().wait()

    def step(k):
        @pl.when(k < chunks)
        def _():
            for d in far_first:
                sending(k, d).wait_recv()
                forwarding(k, d).start()

        @pl.when(k > 0)
        def _():
            last = k - 1
            eig_copy(last).wait()
            for d in far_first:
                forwarding(last, d).wait_recv()
            left = exch[:, :, cols(last)].reshape(n * rows, width)

            def tile(j):
                at = span(j * TILE, TILE, TILE)
                total[:, at] += jnp.dot(
                    left, eig[span(last * width, width, 16), at],
                    preferred_element_type=jnp.float32)

            loop(half // TILE, tile)

    loop(chunks + 1, step)

    def drain(k):
        for d in far_first:
            sending(k, d).wait_send()
            forwarding(k, d).wait_send()

    if not with_tail:
        loop(chunks, drain)
        return

    share = n * rows // groups
    own_rows = span(rank * share, share, share)

    def summing(e):
        to, device = peer(e)
        return pltpu.make_async_remote_copy(
            src_ref=total.at[span(to * share, share, share)], dst_ref=sums.at[e - 1],
            send_sem=sum_send.at[e - 1], recv_sem=sum_recv.at[e - 1],
            device_id=device, device_id_type=MESH)

    def sharing(e):
        return pltpu.make_async_remote_copy(
            src_ref=coef.at[own_rows], dst_ref=coef.at[own_rows],
            send_sem=all_send.at[e - 1], recv_sem=all_recv.at[e - 1],
            device_id=peer(e)[1], device_id_type=MESH)

    for e in range(groups - 1, 0, -1):
        summing(e).start()
    loop(chunks, drain)
    acc = total[own_rows, :]
    for e in range(1, groups):
        summing(e).wait_recv()
        acc = acc + sums[e - 1]
    coef[own_rows, :] = acc.astype(jnp.bfloat16)
    for e in range(groups - 1, 0, -1):
        sharing(e).start()
    for e in range(1, groups):
        summing(e).wait_send()
    for e in range(1, groups):
        sharing(e).wait()

    block = 2 * half // groups
    per_half = groups // 2
    at = span((rank % per_half) * block, block, block)
    sibling = pltpu.make_async_remote_copy(
        src_ref=coef.at[:, at], dst_ref=other, send_sem=sib_send, recv_sem=sib_recv,
        device_id={"sub": 1 - c}, device_id_type=MESH)
    sibling.start()
    coef_out[...] = coef[...]
    sibling.wait()
    here = rank // per_half == c

    @pl.when(here)
    def _():
        block_out[...] = coef[:, at]

    @pl.when(jnp.logical_not(here))
    def _():
        block_out[...] = other[...]


def projected(densities, eigvecs, n, n_ga):
    rows = densities.shape[0]
    _, depth, half = eigvecs.shape
    groups = n * n_ga
    pairs = n * rows
    chunks = depth // WIDTH if depth % WIDTH == 0 else 1
    with_tail = (
        pairs % (16 * groups) == 0 and (2 * half) % (128 * groups) == 0 and groups % 2 == 0
    )
    if depth % 128:
        densities = densities.reshape(rows, n, depth).transpose(1, 0, 2)
    dma = pltpu.SemaphoreType.DMA
    any_space = pl.BlockSpec(memory_space=pl.ANY)
    vmem = pl.BlockSpec(memory_space=pltpu.VMEM)
    scratch = [pltpu.VMEM((depth, half), jnp.bfloat16), pltpu.VMEM((n, rows, depth), jnp.bfloat16)]
    sems = [dma((chunks,)), dma] + [dma((chunks, n - 1))] * 4
    if with_tail:
        share, block = pairs // groups, 2 * half // groups
        scratch += [
            pltpu.VMEM((pairs, half), jnp.float32),
            pltpu.VMEM((groups - 1, share, half), jnp.float32),
            pltpu.VMEM((pairs, half), jnp.bfloat16),
            pltpu.VMEM((pairs, block), jnp.bfloat16),
        ]
        sems += [dma((groups - 1,))] * 4 + [dma, dma]
        out_shape = (
            jax.ShapeDtypeStruct((pairs, half), jnp.bfloat16),
            jax.ShapeDtypeStruct((pairs, block), jnp.bfloat16),
        )
        out_specs = (vmem, vmem)
    else:
        out_shape = jax.ShapeDtypeStruct((pairs, half), jnp.float32)
        out_specs = vmem
    return with_tail, pl.pallas_call(
        functools.partial(kernel, n, n_ga, chunks, with_tail),
        out_shape=out_shape,
        in_specs=[any_space, any_space],
        out_specs=out_specs,
        scratch_shapes=scratch + sems,
        compiler_params=pltpu.CompilerParams(
            collective_id=0, has_side_effects=True, vmem_limit_bytes=56 * 1024 * 1024),
        cost_estimate=pl.CostEstimate(
            flops=2 * pairs * depth * half, transcendentals=0,
            bytes_accessed=2 * depth * (half + pairs)),
    )(densities, eigvecs)


def on_device(densities, eigvecs, energies, frequencies):
    n, n_ga = lax.axis_size("pair"), lax.axis_size("ga")
    total_pairs = n * densities.shape[0]
    done, got = projected(densities, eigvecs, n, n_ga)
    if done:
        coefficients, columns = got
    else:
        coefficients = lax.psum(got, ("pair", "ga")).astype(jnp.bfloat16)
        half = coefficients.shape[1]
        width = 2 * half // (n * n_ga)
        start = (lax.axis_index("pair") * n_ga + lax.axis_index("ga")) * width
        swapped = lax.ppermute(coefficients, "sub", [(0, 1), (1, 0)])
        first = lax.axis_index("sub") == 0
        whole = jnp.concatenate(
            [jnp.where(first, coefficients, swapped), jnp.where(first, swapped, coefficients)], axis=1)
        columns = lax.dynamic_slice_in_dim(whole, start, width, 1)
    squared = energies * energies
    factor = (
        2.0 * energies[None, :] / (squared[None, :] + frequencies[:, None] * frequencies[:, None])
    )
    weighted = (factor[:, :, None] * columns.astype(jnp.float32)[None, :, :]).astype(jnp.bfloat16)
    result = jnp.einsum("ps,wpt->wst", coefficients, weighted, preferred_element_type=jnp.float32)
    return result * (-1.0 / total_pairs)


def solution(mesh):
    placed = (P(("grp", "pair"), "ga"), P("ga", "pair", "sub"), P("grp"), P())
    return jax.shard_map(
        on_device,
        mesh=mesh,
        in_specs=placed,
        out_specs=P("grp", "sub", ("pair", "ga")),
        check_vma=False,
    )
```

time: 160 us -> 85.4 us (0.53)
  blocking collectives: 135 us -> 0 us
  Pallas kernels: 0 us -> 73.7 us
  matrix products: 15.1 us -> 3.58 us
    all_to_all x1 -> x0, blocking collectives: 93.6 us -> none  [on_device(): lax.all_to_all(densities, 'pair', split_axis=1, concat_axis=0, tiled=True)]
    pallas_call x0 -> x1, Pallas kernels: none -> 73.7 us  [projected(): pl.pallas_call(functools.partial(kernel, n, n_ga, chunks, with_tail), out...]
    psum x1 -> x0, blocking collectives: 41.6 us -> none  [on_device(): coefficients = lax.psum(partial_value, ('pair', 'ga')).astype(jnp.bfloat16)]
    dot_general x1 -> x0, matrix products: 12.4 us -> none  [on_device(): jnp.dot(exchanged, local_basis, preferred_element_type=jnp.float32)]
    all_to_all x1 -> x0, local copies, waits for them, and re-layouts: 2.37 us -> none  [on_device(): lax.all_to_all(densities, 'pair', split_axis=1, concat_axis=0, tiled=True)]
  transfers between devices with their start and end apart: 1 -> 0, of which waited for: 1 -> 0; matrix products, arithmetic and copies ran while one was open for 0% -> 0% of each run, Pallas kernels for 0% -> 0%
where the time goes in v1:
time: 85.4 us; the launch traced here: 85.1 us
  Pallas kernels  73.7 us (86%)
  local copies, waits for them, and re-layouts  6.3 us (7%)
  matrix products  3.58 us (4%)
  other arithmetic  1.46 us (2%)
    pallas_call x1, Pallas kernels, projected(): pl.pallas_call(functools.partial(kernel, n, n_ga, chunks, with_tail), out...  73.7 us
    mul x1, local copies, waits for them, and re-layouts, on_device(): return result * (-1.0 / total_pairs)  5.36 us
    dot_general x1, matrix products, on_device(): jnp.einsum('ps,wpt->wst', coefficients, weighted, preferred_element_type=...  3.58 us

profile of v1, /device:TPU:0, one launch (start us, length us, event | category | flops | bytes accessed | tf_op | source)
XLA Modules:
  0.0 85.1 jit_solution(5891260007290602926)
XLA Ops:
  0.0 0.7 mul.39
  0.7 0.7 broadcast_multiply_fusion
  1.4 0.1 add_divide_fusion
  1.5 73.7 %shard_map.46 = (bf16[128,1024]{1,0:T(8,128)(2,1)}, bf16[128,256]{1,0:T(8,128)(2,1)}) custom-call(bf16[32,61440]{1,0:T(8,128)(2,1)} %dens.1, bf16[1,15360,1024]{2,1,0:T(8,128)(2,1)} %basis.1), custom_call_target="tpu_custom_call" | custom-call | flops 4026531840 | bytes 35389440 | tf_op jit(solution)/shard_map/pallas_call | solution.py:220
  75.2 0.9 %copy.5 = f32[128,256]{0,1:T(8,128)S(1)} copy(bf16[128,256]{1,0:T(8,128)(2,1)} %get-tuple-element.7) | data formatting | bytes 196608 | tf_op jit(solution)/shard_map/convert_element_type | solution.py:254
  76.2 3.6 %multiply_bitcast_fusion = f32[4,1024,256]{1,2,0:T(8,128)} fusion(bf16[128,1024]{1,0:T(8,128)(2,1)} %get-tuple-element.8, f32[128,256]{0,1:T(8,128)S(1)} %copy.5, f32[4,128]{1,0:T(4,128)S(1)} %add_divide_fusion), kind=kOutput, calls=%fused_computation | convolution fusion | flops 269746176 | bytes 4589568 | tf_op jit(solution)/shard_map/ps,wpt->wst/dot_general | solution.py:255
  79.7 5.4 %copy.6 = f32[4,1024,256]{2,1,0:T(8,128)} copy(f32[4,1024,256]{1,2,0:T(8,128)} %multiply_bitcast_fusion) | data formatting | bytes 8388608 | tf_op jit(solution)/shard_map/mul | solution.py:256

commit v2 on v1

v2 whole, which is shorter than its diff:
```python
import functools

import jax
import jax.numpy as jnp
from jax import lax
from jax.experimental import pallas as pl
from jax.experimental.pallas import tpu as pltpu
from jax.sharding import PartitionSpec as P

MESH = pl.DeviceIdType.MESH
WIDTH = 1536
TILE = 256
STAGES = 2
AHEAD = 4


def flipped(index, bits):
    bit = 1
    while bit <= bits:
        if bits & bit:
            index = index + bit - 2 * bit * ((index // bit) % 2)
        bit *= 2
    return index


def span(start, size, unit):
    return pl.ds(pl.multiple_of(start, unit), size)


def plain_kernel(n, n_ga, dens, basis, total, eig, exch, eig_sem, own_sem, send, recv, fwd_send, fwd_recv):
    z, x, c = lax.axis_index("pair"), lax.axis_index("ga"), lax.axis_index("sub")
    depth, half = eig.shape
    rows = exch.shape[1]
    part = rows // 2
    chunks = eig_sem.shape[0]
    width = depth // chunks
    groups = n * n_ga
    rank = z * n_ga + x
    pieced = len(dens.shape) == 3

    def cols(k):
        return slice(None) if chunks == 1 else span(k * width, width, 128)

    def eig_copy(k):
        at = span(k * width, width, 16)
        return pltpu.make_async_copy(basis.at[0, at], eig.at[at], eig_sem.at[k])

    def own_copy():
        src = dens.at[z] if pieced else dens.at[:, span(z * depth, depth, 128)]
        return pltpu.make_async_copy(src, exch.at[z], own_sem)

    mine = span(c * part, part, part)

    def sending(k, d):
        to = flipped(z, d)
        if pieced:
            src = dens.at[to, mine]
        else:
            src = dens.at[mine, span(to * depth + k * width, width, 128)]
        return pltpu.make_async_remote_copy(
            src_ref=src, dst_ref=exch.at[z, mine, cols(k)],
            send_sem=send.at[k, d - 1], recv_sem=recv.at[k, d - 1],
            device_id={"pair": to}, device_id_type=MESH)

    def forwarding(k, d):
        here = exch.at[flipped(z, d), mine, cols(k)]
        return pltpu.make_async_remote_copy(
            src_ref=here, dst_ref=here,
            send_sem=fwd_send.at[k, d - 1], recv_sem=fwd_recv.at[k, d - 1],
            device_id={"sub": 1 - c}, device_id_type=MESH)

    def peer(e):
        to = flipped(rank, e)
        return to, {"pair": to // n_ga, "ga": to % n_ga}

    def loop(count, body):
        lax.fori_loop(0, count, lambda i, _: (body(i), 0)[1], 0)

    loop(chunks, lambda k: eig_copy(k).start())
    own_copy().start()

    barrier = pltpu.get_barrier_semaphore()
    greeted = range(n_ga, groups, n_ga)
    for e in greeted:
        pl.semaphore_signal(barrier, inc=1, device_id=peer(e)[1], device_id_type=MESH)
    pl.semaphore_signal(barrier, inc=1, device_id={"sub": 1 - c}, device_id_type=MESH)
    pl.semaphore_wait(barrier, len(greeted) + 1)

    far_first = range(n - 1, 0, -1)

    def send_chunk(k):
        for d in far_first:
            sending(k, d).start()

    loop(chunks, send_chunk)
    total[...] = jnp.zeros_like(total)
    own_copy().wait()

    def step(k):
        @pl.when(k < chunks)
        def _():
            for d in far_first:
                sending(k, d).wait_recv()
                forwarding(k, d).start()

        @pl.when(k > 0)
        def _():
            last = k - 1
            eig_copy(last).wait()
            for d in far_first:
                forwarding(last, d).wait_recv()
            left = exch[:, :, cols(last)].reshape(n * rows, width)

            def tile(j):
                at = span(j * TILE, TILE, TILE)
                total[:, at] += jnp.dot(
                    left, eig[span(last * width, width, 16), at],
                    preferred_element_type=jnp.float32)

            loop(half // TILE, tile)

    loop(chunks + 1, step)

    def drain(k):
        for d in far_first:
            sending(k, d).wait_send()
            forwarding(k, d).wait_send()

    loop(chunks, drain)


def fused_kernel(
    n, n_ga, chunks, dens, basis, coef_out, block_out, eig, exch, total, x_in, z_in, coef, other,
    eig_sem, own_sem, send, recv, fwd_send, fwd_recv,
    x_send, x_recv, z_send, z_recv, all_send, all_recv, sib_send, sib_recv,
):
    z, x, c = lax.axis_index("pair"), lax.axis_index("ga"), lax.axis_index("sub")
    depth, half = eig.shape
    _, stages, part, _ = coef.shape
    reach = depth // 2
    width = reach // chunks
    steps = stages * chunks
    groups = n * n_ga
    rank = z * n_ga + x
    share = n // n_ga
    strip = half // n
    far_first = range(n - 1, 0, -1)

    def eig_copy(k, h):
        at = span(h * reach + k * width, width, 256)
        return pltpu.make_async_copy(basis.at[0, at], eig.at[at], eig_sem.at[k, h])

    def own_copy():
        return pltpu.make_async_copy(dens.at[:, span(z * depth, depth, 256)], exch.at[z], own_sem)

    def piece(g):
        s, k = divmod(g, chunks)
        return pl.ds(s * part, part), c * reach + k * width

    def sending(g, d):
        to = flipped(z, d)
        rows, at = piece(g)
        return pltpu.make_async_remote_copy(
            src_ref=dens.at[rows, span(to * depth + at, width, 256)],
            dst_ref=exch.at[z, rows, span(at, width, 256)],
            send_sem=send.at[g, d - 1], recv_sem=recv.at[g, d - 1],
            device_id={"pair": to}, device_id_type=MESH)

    def forwarding(g, d):
        rows, at = piece(g)
        here = exch.at[flipped(z, d), rows, span(at, width, 256)]
        return pltpu.make_async_remote_copy(
            src_ref=here, dst_ref=here,
            send_sem=fwd_send.at[g, d - 1], recv_sem=fwd_recv.at[g, d - 1],
            device_id={"sub": 1 - c}, device_id_type=MESH)

    def peer(e):
        to = flipped(rank, e)
        return {"pair": to // n_ga, "ga": to % n_ga}

    def kept(to):
        return pl.ds(to * share, share)

    def strip_of(to):
        return span(to * strip, strip, strip)

    def x_sum(s, e):
        to = flipped(x, e)
        return pltpu.make_async_remote_copy(
            src_ref=total.at[s, kept(to)], dst_ref=x_in.at[s, e - 1],
            send_sem=x_send.at[s, e - 1], recv_sem=x_recv.at[s, e - 1],
            device_id={"ga": to}, device_id_type=MESH)

    def z_sum(s, d):
        to = flipped(z, d)
        return pltpu.make_async_remote_copy(
            src_ref=total.at[s, kept(x), :, strip_of(to)], dst_ref=z_in.at[s, d - 1],
            send_sem=z_send.at[s, d - 1], recv_sem=z_recv.at[s, d - 1],
            device_id={"pair": to}, device_id_type=MESH)

    def sharing(s, e):
        here = coef.at[kept(x), s, :, strip_of(z)]
        return pltpu.make_async_remote_copy(
            src_ref=here, dst_ref=here,
            send_sem=all_send.at[s, e - 1], recv_sem=all_recv.at[s, e - 1],
            device_id=peer(e), device_id_type=MESH)

    def begin_x(s):
        for e in range(1, n_ga):
            x_sum(s, e).start()

    def begin_z(s):
        acc = total[s, kept(x)]
        for e in range(1, n_ga):
            x_sum(s, e).wait_recv()
            acc = acc + x_in[s, e - 1]
        total[s, kept(x)] = acc
        for d in far_first:
            z_sum(s, d).start()

    def begin_sharing(s):
        acc = total[s, kept(x), :, strip_of(z)]
        for d in far_first:
            z_sum(s, d).wait_recv()
            acc = acc + z_in[s, d - 1]
        coef[kept(x), s, :, strip_of(z)] = acc.astype(jnp.bfloat16)
        for e in range(groups - 1, 0, -1):
            sharing(s, e).start()

    def multiply(g):
        s, k = divmod(g, chunks)
        if s == 0:
            for h in range(2):
                eig_copy(k, h).wait()
        for d in far_first:
            forwarding(g, d).wait_recv()

        def tile(j, carry):
            at = span(j * TILE, TILE, TILE)
            acc = 0.0
            for h in range(2):
                deep = pl.ds(h * reach + k * width, width)
                left = exch[:, pl.ds(s * part, part), deep].reshape(n * part, width)
                acc += jnp.dot(left, eig[deep, at], preferred_element_type=jnp.float32)
            acc = acc.reshape(n, part, TILE)
            if k:
                acc += total[s, :, :, at]
            total[s, :, :, at] = acc
            return carry

        lax.fori_loop(0, half // TILE, tile, 0)

    for k in range(chunks):
        for h in range(2):
            eig_copy(k, h).start()
    own_copy().start()

    barrier = pltpu.get_barrier_semaphore()
    for e in range(1, groups):
        pl.semaphore_signal(barrier, inc=1, device_id=peer(e), device_id_type=MESH)
    pl.semaphore_signal(barrier, inc=1, device_id={"sub": 1 - c}, device_id_type=MESH)
    pl.semaphore_wait(barrier, groups)

    for g in range(min(AHEAD, steps)):
        for d in far_first:
            sending(g, d).start()
    own_copy().wait()

    after = {}
    for s in range(stages - 1):
        done = (s + 1) * chunks
        gap = max(1, (chunks - 1) // 2)
        after.setdefault(done, []).append((begin_x, s))
        after.setdefault(done + gap, []).append((begin_z, s))
        after.setdefault(done + 2 * gap, []).append((begin_sharing, s))

    for g in range(steps + 1):
        if g < steps:
            for d in far_first:
                sending(g, d).wait_recv()
                forwarding(g, d).start()
            if g + AHEAD < steps:
                for d in far_first:
                    sending(g + AHEAD, d).start()
        if g > 0:
            multiply(g - 1)
        for act, s in after.get(g, []):
            act(s)

    last = stages - 1
    begin_x(last)
    for g in range(steps):
        for d in far_first:
            sending(g, d).wait_send()
            forwarding(g, d).wait_send()
    begin_z(last)
    begin_sharing(last)
    for s in range(stages):
        for e in range(1, n_ga):
            x_sum(s, e).wait_send()
        for d in far_first:
            z_sum(s, d).wait_send()
    for s in range(stages):
        for e in range(1, groups):
            sharing(s, e).wait()

    block = 2 * half // groups
    per_half = groups // 2
    at = span((rank % per_half) * block, block, block)
    sibling = pltpu.make_async_remote_copy(
        src_ref=coef.at[:, :, :, at], dst_ref=other, send_sem=sib_send, recv_sem=sib_recv,
        device_id={"sub": 1 - c}, device_id_type=MESH)
    sibling.start()
    coef_out[...] = coef[...]
    sibling.wait()
    here = rank // per_half == c

    @pl.when(here)
    def _():
        block_out[...] = coef[:, :, :, at]

    @pl.when(jnp.logical_not(here))
    def _():
        block_out[...] = other[...]


def final_kernel(scale, coef, columns, energies, frequencies, out, turned):
    w = pl.program_id(0)

    @pl.when(w == 0)
    def _():
        turned[...] = coef[...].T

    pairs, width = columns.shape
    energy = jnp.broadcast_to(energies[...], (128, pairs)).T
    frequency = frequencies[w]
    factor = 2.0 * energy / (energy * energy + frequency * frequency)
    for i in range(0, width, 128):
        weighted = (factor * columns[:, i:i + 128].astype(jnp.float32)).astype(jnp.bfloat16)
        if i % 256 == 0:
            held = [weighted]
        else:
            held.append(weighted)
        if i % 256 == 128 or i + 128 == width:
            start = i + 128 - 128 * len(held)
            right = jnp.concatenate(held, axis=1)
            value = jnp.dot(turned[...], right, preferred_element_type=jnp.float32)
            out[0, :, start:i + 128] = value * scale


def plain(densities, eigvecs, n, n_ga):
    rows = densities.shape[0]
    _, depth, half = eigvecs.shape
    chunks = depth // WIDTH if depth % WIDTH == 0 else 1
    if depth % 128:
        densities = densities.reshape(rows, n, depth).transpose(1, 0, 2)
    dma = pltpu.SemaphoreType.DMA
    any_space = pl.BlockSpec(memory_space=pl.ANY)
    return pl.pallas_call(
        functools.partial(plain_kernel, n, n_ga),
        out_shape=jax.ShapeDtypeStruct((n * rows, half), jnp.float32),
        in_specs=[any_space, any_space],
        out_specs=pl.BlockSpec(memory_space=pltpu.VMEM),
        scratch_shapes=[
            pltpu.VMEM((depth, half), jnp.bfloat16),
            pltpu.VMEM((n, rows, depth), jnp.bfloat16),
            dma((chunks,)), dma,
        ] + [dma((chunks, n - 1))] * 4,
        compiler_params=pltpu.CompilerParams(
            collective_id=0, has_side_effects=True, vmem_limit_bytes=56 * 1024 * 1024),
    )(densities, eigvecs)


def fused(densities, eigvecs, n, n_ga):
    rows = densities.shape[0]
    _, depth, half = eigvecs.shape
    groups = n * n_ga
    chunks = depth // (2 * WIDTH)
    part, block, share = rows // STAGES, 2 * half // groups, n // n_ga
    dma = pltpu.SemaphoreType.DMA
    any_space = pl.BlockSpec(memory_space=pl.ANY)
    vmem = pl.BlockSpec(memory_space=pltpu.VMEM)
    coef_shape, block_shape = (n, STAGES, part, half), (n, STAGES, part, block)
    coef, columns = pl.pallas_call(
        functools.partial(fused_kernel, n, n_ga, chunks),
        out_shape=(
            jax.ShapeDtypeStruct(coef_shape, jnp.bfloat16),
            jax.ShapeDtypeStruct(block_shape, jnp.bfloat16),
        ),
        in_specs=[any_space, any_space],
        out_specs=(vmem, vmem),
        scratch_shapes=[
            pltpu.VMEM((depth, half), jnp.bfloat16),
            pltpu.VMEM((n, rows, depth), jnp.bfloat16),
            pltpu.VMEM((STAGES, n, part, half), jnp.float32),
            pltpu.VMEM((STAGES, n_ga - 1, share, part, half), jnp.float32),
            pltpu.VMEM((STAGES, n - 1, share, part, half // n), jnp.float32),
            pltpu.VMEM(coef_shape, jnp.bfloat16),
            pltpu.VMEM(block_shape, jnp.bfloat16),
            dma((chunks, 2)), dma,
        ] + [dma((STAGES * chunks, n - 1))] * 4 + [
            dma((STAGES, n_ga - 1)), dma((STAGES, n_ga - 1)),
            dma((STAGES, n - 1)), dma((STAGES, n - 1)),
            dma((STAGES, groups - 1)), dma((STAGES, groups - 1)), dma, dma,
        ],
        compiler_params=pltpu.CompilerParams(
            collective_id=0, has_side_effects=True, vmem_limit_bytes=56 * 1024 * 1024),
        cost_estimate=pl.CostEstimate(
            flops=2 * n * rows * depth * half, transcendentals=0,
            bytes_accessed=2 * depth * (half + n * rows)),
    )(densities, eigvecs)
    return coef.reshape(n * rows, half), columns.reshape(n * rows, block)


def final(coef, columns, energies, frequencies):
    pairs, half = coef.shape
    block = columns.shape[1]
    count = frequencies.shape[0]
    return pl.pallas_call(
        functools.partial(final_kernel, -1.0 / pairs),
        grid=(count,),
        out_shape=jax.ShapeDtypeStruct((count, half, block), jnp.float32),
        in_specs=[
            pl.BlockSpec((pairs, half), lambda w: (0, 0)),
            pl.BlockSpec((pairs, block), lambda w: (0, 0)),
            pl.BlockSpec((1, pairs), lambda w: (0, 0)),
            pl.BlockSpec(memory_space=pltpu.SMEM),
        ],
        out_specs=pl.BlockSpec((1, half, block), lambda w: (w, 0, 0)),
        scratch_shapes=[pltpu.VMEM((half, pairs), jnp.bfloat16)],
        compiler_params=pltpu.CompilerParams(vmem_limit_bytes=16 * 1024 * 1024),
    )(coef, columns, energies.reshape(1, pairs), frequencies)


def on_device(densities, eigvecs, energies, frequencies):
    n, n_ga = lax.axis_size("pair"), lax.axis_size("ga")
    rows, depth, half = densities.shape[0], eigvecs.shape[1], eigvecs.shape[2]
    groups = n * n_ga
    fits = (
        depth % (2 * WIDTH) == 0 and rows % (16 * STAGES) == 0 and n % n_ga == 0
        and half % (128 * n) == 0 and (2 * half) % (128 * groups) == 0 and groups % 2 == 0
    )
    if fits:
        coefficients, columns = fused(densities, eigvecs, n, n_ga)
        return final(coefficients, columns, energies, frequencies)
    partial_value = plain(densities, eigvecs, n, n_ga)
    coefficients = lax.psum(partial_value, ("pair", "ga")).astype(jnp.bfloat16)
    width = 2 * half // groups
    start = (lax.axis_index("pair") * n_ga + lax.axis_index("ga")) * width
    swapped = lax.ppermute(coefficients, "sub", [(0, 1), (1, 0)])
    first = lax.axis_index("sub") == 0
    whole = jnp.concatenate(
        [jnp.where(first, coefficients, swapped), jnp.where(first, swapped, coefficients)], axis=1)
    columns = lax.dynamic_slice_in_dim(whole, start, width, 1)
    squared = energies * energies
    factor = (
        2.0 * energies[None, :] / (squared[None, :] + frequencies[:, None] * frequencies[:, None])
    )
    weighted = (factor[:, :, None] * columns.astype(jnp.float32)[None, :, :]).astype(jnp.bfloat16)
    result = jnp.einsum("ps,wpt->wst", coefficients, weighted, preferred_element_type=jnp.float32)
    return result * (-1.0 / (n * rows))


def solution(mesh):
    placed = (P(("grp", "pair"), "ga"), P("ga", "pair", "sub"), P("grp"), P())
    return jax.shard_map(
        on_device,
        mesh=mesh,
        in_specs=placed,
        out_specs=P("grp", "sub", ("pair", "ga")),
        check_vma=False,
    )
```

time: 85.4 us -> 77.1 us (0.903)
  local copies, waits for them, and re-layouts: 6.3 us -> 1.79 us
  matrix products: 3.58 us -> 0 us
  other arithmetic: 1.46 us -> 0 us
  Pallas kernels: 73.7 us -> 75.1 us
    mul x1 -> x0, local copies, waits for them, and re-layouts: 5.36 us -> none  [on_device(): return result * (-1.0 / total_pairs)]
    dot_general x1 -> x0, matrix products: 3.58 us -> none  [on_device(): jnp.einsum('ps,wpt->wst', coefficients, weighted, preferred_element_type=...]
    unnamed x0 -> x8, local copies, waits for them, and re-layouts: none -> 1.79 us
    mul x2 -> x0, other arithmetic: 1.39 us -> none  [the longest x1 0.73 us: on_device(): frequencies[:, None] * frequencies[:, None]]
    pallas_call x1 -> x2, Pallas kernels: 73.7 us -> 75.1 us  [the longest x1 71.3 us: fused(): pl.pallas_call(functools.partial(fused_kernel, n, n_ga, chunks), out_shap...]
    convert_element_type x1 -> x0, local copies, waits for them, and re-layouts: 0.94 us -> none  [on_device(): columns.astype(jnp.float32)[None, :, :]]
where the time goes in v2:
time: 77.1 us; the launch traced here: 76.9 us
  Pallas kernels  75.1 us (97%)
  local copies, waits for them, and re-layouts  1.79 us (2%)
    pallas_call x1, Pallas kernels, fused(): pl.pallas_call(functools.partial(fused_kernel, n, n_ga, chunks), out_shap...  71.3 us
    pallas_call x1, Pallas kernels, final(): pl.pallas_call(functools.partial(final_kernel, -1.0 / pairs), grid=(count...  3.77 us
    unnamed x8, local copies, waits for them, and re-layouts  1.79 us

profile of v2, /device:TPU:0, one launch (start us, length us, event | category | flops | bytes accessed | tf_op | source)
XLA Modules:
  0.0 76.9 jit_solution(1897175013861698188)
XLA Ops:
  0.0 0.0 copy-start.2
  0.0 0.0 copy-start.3
  0.0 71.3 %shard_map.46 = (bf16[4,2,16,1024]{3,2,1,0:T(8,128)(2,1)}, bf16[4,2,16,256]{3,2,1,0:T(8,128)(2,1)}) custom-call(bf16[32,61440]{1,0:T(8,128)(2,1)} %dens.1, bf16[1,15360,1024]{2,1,0:T(8,128)(2,1)} %basis.1), custom_call_target="tpu_custom_call" | custom-call | flops 4026531840 | bytes 35389440 | tf_op jit(solution)/shard_map/pallas_call | solution.py:384
  71.3 0.0 copy-done.2
  71.4 0.0 copy-done.3
  71.4 0.0 copy-start
  71.4 0.9 %copy-done = bf16[4,2,16,1024]{3,2,1,0:T(8,128)(2,1)S(1)} copy-done((bf16[4,2,16,1024]{3,2,1,0:T(8,128)(2,1)S(1)}, bf16[4,2,16,1024]{3,2,1,0:T(8,128)(2,1)}, u32[]{:S(2)}) %copy-start) | copy-done | bytes 262168
  72.3 0.0 copy-start.1
  72.3 0.8 %copy-done.1 = bf16[4,2,16,256]{3,2,1,0:T(8,128)(2,1)S(1)} copy-done((bf16[4,2,16,256]{3,2,1,0:T(8,128)(2,1)S(1)}, bf16[4,2,16,256]{3,2,1,0:T(8,128)(2,1)}, u32[]{:S(2)}) %copy-start.1) | copy-done | bytes 65560
  73.2 3.8 %shard_map.47 = f32[4,1024,256]{2,1,0:T(8,128)} custom-call(bf16[128,1024]{1,0:T(8,128)(2,1)S(1)} %bitcast.3, bf16[128,256]{1,0:T(8,128)(2,1)S(1)} %bitcast.4, f32[1,128]{1,0:T(1,128)S(1)} %bitcast.5, f32[4]{0:T(128)S(1)} %copy-done.3), custom_call_target="tpu_custom_call" | custom-call | tf_op jit(solution)/shard_map/pallas_call | solution.py:419
Async XLA Ops:
  0.0 71.3 %copy-start.2 = (f32[128]{0:T(128)S(1)}, f32[128]{0:T(128)}, u32[]{:S(2)}) copy-start(f32[128]{0:T(128)} %param.6) | copy-start | bytes 1540
  0.0 71.4 %copy-start.3 = (f32[4]{0:T(128)S(1)}, f32[4]{0:T(128)}, u32[]{:S(2)}) copy-start(f32[4]{0:T(128)} %frequencies.1) | copy-start | bytes 52
  71.4 1.0 %copy-start = (bf16[4,2,16,1024]{3,2,1,0:T(8,128)(2,1)S(1)}, bf16[4,2,16,1024]{3,2,1,0:T(8,128)(2,1)}, u32[]{:S(2)}) copy-start(bf16[4,2,16,1024]{3,2,1,0:T(8,128)(2,1)} %get-tuple-element.7) | copy-start | bytes 786436
  72.3 0.8 %copy-start.1 = (bf16[4,2,16,256]{3,2,1,0:T(8,128)(2,1)S(1)}, bf16[4,2,16,256]{3,2,1,0:T(8,128)(2,1)}, u32[]{:S(2)}) copy-start(bf16[4,2,16,256]{3,2,1,0:T(8,128)(2,1)} %get-tuple-element.8) | copy-start | bytes 196612

commit v3 on v2

--- a/solution.py
+++ b/solution.py
@@ -145,6 +145,8 @@
     share = n // n_ga
     strip = half // n
     far_first = range(n - 1, 0, -1)
+    all_far_first = range(n - 1, -1, -1)
+    crosses = (rank // n + c) % 2
 
     def eig_copy(k, h):
         at = span(h * reach + k * width, width, 256)
@@ -184,11 +186,11 @@
     def strip_of(to):
         return span(to * strip, strip, strip)
 
-    def x_sum(s, e):
-        to = flipped(x, e)
-        return pltpu.make_async_remote_copy(
-            src_ref=total.at[s, kept(to)], dst_ref=x_in.at[s, e - 1],
-            send_sem=x_send.at[s, e - 1], recv_sem=x_recv.at[s, e - 1],
+    def x_sum(s, e, d):
+        to, at = flipped(x, e), strip_of(flipped(z, d))
+        return pltpu.make_async_remote_copy(
+            src_ref=total.at[s, kept(to), :, at], dst_ref=x_in.at[s, e - 1, :, :, at],
+            send_sem=x_send.at[s, e - 1, d], recv_sem=x_recv.at[s, e - 1, d],
             device_id={"ga": to}, device_id_type=MESH)
 
     def z_sum(s, d):
@@ -205,18 +207,34 @@
             send_sem=all_send.at[s, e - 1], recv_sem=all_recv.at[s, e - 1],
             device_id=peer(e), device_id_type=MESH)
 
+    def crossing(s):
+        to = c * n + z
+        return pltpu.make_async_remote_copy(
+            src_ref=coef.at[kept(x), s, :, strip_of(z)], dst_ref=other.at[kept(x), s],
+            send_sem=sib_send.at[s], recv_sem=sib_recv.at[s, x],
+            device_id={"pair": to // n_ga, "ga": to % n_ga, "sub": 1 - c}, device_id_type=MESH)
+
+    def crossed(s, e):
+        here = other.at[pl.ds(e * share, share), s]
+        return pltpu.make_async_remote_copy(
+            src_ref=here, dst_ref=here, send_sem=sib_send.at[s], recv_sem=sib_recv.at[s, e],
+            device_id={"sub": 1 - c}, device_id_type=MESH)
+
     def begin_x(s):
-        for e in range(1, n_ga):
-            x_sum(s, e).start()
+        for d in all_far_first:
+            for e in range(1, n_ga):
+                x_sum(s, e, d).start()
 
     def begin_z(s):
-        acc = total[s, kept(x)]
-        for e in range(1, n_ga):
-            x_sum(s, e).wait_recv()
-            acc = acc + x_in[s, e - 1]
-        total[s, kept(x)] = acc
-        for d in far_first:
-            z_sum(s, d).start()
+        for d in all_far_first:
+            at = strip_of(flipped(z, d))
+            acc = total[s, kept(x), :, at]
+            for e in range(1, n_ga):
+                x_sum(s, e, d).wait_recv()
+                acc = acc + x_in[s, e - 1, :, :, at]
+            total[s, kept(x), :, at] = acc
+            if d:
+                z_sum(s, d).start()
 
     def begin_sharing(s):
         acc = total[s, kept(x), :, strip_of(z)]
@@ -226,6 +244,7 @@
         coef[kept(x), s, :, strip_of(z)] = acc.astype(jnp.bfloat16)
         for e in range(groups - 1, 0, -1):
             sharing(s, e).start()
+        crossing(s).start()
 
     def multiply(g):
         s, k = divmod(g, chunks)
@@ -236,19 +255,25 @@
             forwarding(g, d).wait_recv()
 
         def tile(j, carry):
-            at = span(j * TILE, TILE, TILE)
+            at = strip_of(j)
             acc = 0.0
             for h in range(2):
                 deep = pl.ds(h * reach + k * width, width)
                 left = exch[:, pl.ds(s * part, part), deep].reshape(n * part, width)
                 acc += jnp.dot(left, eig[deep, at], preferred_element_type=jnp.float32)
-            acc = acc.reshape(n, part, TILE)
+            acc = acc.reshape(n, part, strip)
             if k:
                 acc += total[s, :, :, at]
             total[s, :, :, at] = acc
             return carry
 
-        lax.fori_loop(0, half // TILE, tile, 0)
+        if g < steps - 1:
+            lax.fori_loop(0, n, tile, 0)
+        else:
+            for d in all_far_first:
+                tile(flipped(z, d), 0)
+                for e in range(1, n_ga):
+                    x_sum(s, e, d).start()
 
     for k in range(chunks):
         for h in range(2):
@@ -259,7 +284,18 @@
     for e in range(1, groups):
         pl.semaphore_signal(barrier, inc=1, device_id=peer(e), device_id_type=MESH)
     pl.semaphore_signal(barrier, inc=1, device_id={"sub": 1 - c}, device_id_type=MESH)
-    pl.semaphore_wait(barrier, groups)
+    pl.semaphore_signal(
+        barrier, inc=1, device_id_type=MESH,
+        device_id={"pair": (c * n + z) // n_ga, "ga": (c * n + z) % n_ga, "sub": 1 - c})
+
+    @pl.when(crosses == 1)
+    def _():
+        for e in range(n_ga):
+            pl.semaphore_signal(
+                barrier, inc=1, device_id={"pair": rank % n, "ga": e, "sub": 1 - c},
+                device_id_type=MESH)
+
+    pl.semaphore_wait(barrier, groups + 1 + n_ga * crosses)
 
     for g in range(min(AHEAD, steps)):
         for d in far_first:
@@ -288,64 +324,58 @@
             act(s)
 
     last = stages - 1
-    begin_x(last)
+    begin_z(last)
     for g in range(steps):
         for d in far_first:
             sending(g, d).wait_send()
             forwarding(g, d).wait_send()
-    begin_z(last)
     begin_sharing(last)
     for s in range(stages):
         for e in range(1, n_ga):
-            x_sum(s, e).wait_send()
+            for d in all_far_first:
+                x_sum(s, e, d).wait_send()
         for d in far_first:
             z_sum(s, d).wait_send()
     for s in range(stages):
         for e in range(1, groups):
             sharing(s, e).wait()
 
-    block = 2 * half // groups
-    per_half = groups // 2
-    at = span((rank % per_half) * block, block, block)
-    sibling = pltpu.make_async_remote_copy(
-        src_ref=coef.at[:, :, :, at], dst_ref=other, send_sem=sib_send, recv_sem=sib_recv,
-        device_id={"sub": 1 - c}, device_id_type=MESH)
-    sibling.start()
     coef_out[...] = coef[...]
-    sibling.wait()
-    here = rank // per_half == c
-
-    @pl.when(here)
+    for s in range(stages):
+        crossing(s).wait_send()
+
+    @pl.when(crosses == 0)
     def _():
-        block_out[...] = coef[:, :, :, at]
-
-    @pl.when(jnp.logical_not(here))
+        block_out[...] = coef[:, :, :, strip_of(rank % n)]
+
+    @pl.when(crosses == 1)
     def _():
+        for s in range(stages):
+            for e in range(n_ga):
+                crossed(s, e).wait_recv()
         block_out[...] = other[...]
 
 
-def final_kernel(scale, coef, columns, energies, frequencies, out, turned):
-    w = pl.program_id(0)
-
-    @pl.when(w == 0)
-    def _():
-        turned[...] = coef[...].T
-
-    pairs, width = columns.shape
+def final_kernel(scale, coef, columns, energies, frequencies, out, held, done):
+    count, half, width = held.shape
+    pairs = coef.shape[0]
+    turned = coef[...].T
     energy = jnp.broadcast_to(energies[...], (128, pairs)).T
-    frequency = frequencies[w]
-    factor = 2.0 * energy / (energy * energy + frequency * frequency)
-    for i in range(0, width, 128):
-        weighted = (factor * columns[:, i:i + 128].astype(jnp.float32)).astype(jnp.bfloat16)
-        if i % 256 == 0:
-            held = [weighted]
-        else:
-            held.append(weighted)
-        if i % 256 == 128 or i + 128 == width:
-            start = i + 128 - 128 * len(held)
-            right = jnp.concatenate(held, axis=1)
-            value = jnp.dot(turned[...], right, preferred_element_type=jnp.float32)
-            out[0, :, start:i + 128] = value * scale
+    squared = energy * energy
+    wide = columns[...].astype(jnp.float32)
+
+    def copy(w):
+        return pltpu.make_async_copy(held.at[w], out.at[w], done.at[w])
+
+    for w in range(count):
+        frequency = frequencies[w]
+        factor = 2.0 * energy / (squared + frequency * frequency)
+        weighted = [factor * wide[:, i:i + 128] for i in range(0, width, 128)]
+        right = jnp.concatenate(weighted, axis=1).astype(jnp.bfloat16)
+        held[w] = jnp.dot(turned, right, preferred_element_type=jnp.float32) * scale
+        copy(w).start()
+    for w in range(count):
+        copy(w).wait()
 
 
 def plain(densities, eigvecs, n, n_ga):
@@ -399,9 +429,10 @@
             pltpu.VMEM(block_shape, jnp.bfloat16),
             dma((chunks, 2)), dma,
         ] + [dma((STAGES * chunks, n - 1))] * 4 + [
-            dma((STAGES, n_ga - 1)), dma((STAGES, n_ga - 1)),
+            dma((STAGES, n_ga - 1, n)), dma((STAGES, n_ga - 1, n)),
             dma((STAGES, n - 1)), dma((STAGES, n - 1)),
-            dma((STAGES, groups - 1)), dma((STAGES, groups - 1)), dma, dma,
+            dma((STAGES, groups - 1)), dma((STAGES, groups - 1)),
+            dma((STAGES,)), dma((STAGES, n_ga)),
         ],
         compiler_params=pltpu.CompilerParams(
             collective_id=0, has_side_effects=True, vmem_limit_bytes=56 * 1024 * 1024),
@@ -416,18 +447,15 @@
     pairs, half = coef.shape
     block = columns.shape[1]
     count = frequencies.shape[0]
+    vmem = pl.BlockSpec(memory_space=pltpu.VMEM)
     return pl.pallas_call(
         functools.partial(final_kernel, -1.0 / pairs),
-        grid=(count,),
         out_shape=jax.ShapeDtypeStruct((count, half, block), jnp.float32),
-        in_specs=[
-            pl.BlockSpec((pairs, half), lambda w: (0, 0)),
-            pl.BlockSpec((pairs, block), lambda w: (0, 0)),
-            pl.BlockSpec((1, pairs), lambda w: (0, 0)),
-            pl.BlockSpec(memory_space=pltpu.SMEM),
+        in_specs=[vmem, vmem, vmem, pl.BlockSpec(memory_space=pltpu.SMEM)],
+        out_specs=pl.BlockSpec(memory_space=pl.ANY),
+        scratch_shapes=[
+            pltpu.VMEM((count, half, block), jnp.float32), pltpu.SemaphoreType.DMA((count,)),
         ],
-        out_specs=pl.BlockSpec((1, half, block), lambda w: (w, 0, 0)),
-        scratch_shapes=[pltpu.VMEM((half, pairs), jnp.bfloat16)],
         compiler_params=pltpu.CompilerParams(vmem_limit_bytes=16 * 1024 * 1024),
     )(coef, columns, energies.reshape(1, pairs), frequencies)
 
@@ -438,7 +466,7 @@
     groups = n * n_ga
     fits = (
         depth % (2 * WIDTH) == 0 and rows % (16 * STAGES) == 0 and n % n_ga == 0
-        and half % (128 * n) == 0 and (2 * half) % (128 * groups) == 0 and groups % 2 == 0
+        and half % (128 * n) == 0 and n_ga == 2
     )
     if fits:
         coefficients, columns = fused(densities, eigvecs, n, n_ga)

time: 77.1 us -> 74 us (0.960)
  Pallas kernels: 75.1 us -> 71.9 us
    pallas_call x1, Pallas kernels: 71.3 us -> 68.8 us  [fused(): pl.pallas_call(functools.partial(fused_kernel, n, n_ga, chunks), out_shap...]
where the time goes in v3:
time: 74 us; the launch traced here: 73.8 us
  Pallas kernels  71.9 us (97%)
  local copies, waits for them, and re-layouts  1.79 us (2%)
    pallas_call x1, Pallas kernels, fused(): pl.pallas_call(functools.partial(fused_kernel, n, n_ga, chunks), out_shap...  68.8 us
    pallas_call x1, Pallas kernels, final(): pl.pallas_call(functools.partial(final_kernel, -1.0 / pairs), out_shape=j...  3.11 us
    unnamed x8, local copies, waits for them, and re-layouts  1.79 us

profile of v3, /device:TPU:0, one launch (start us, length us, event | category | flops | bytes accessed | tf_op | source)
XLA Modules:
  0.0 73.8 jit_solution(12035856147100453568)
XLA Ops:
  0.0 0.0 copy-start.2
  0.0 0.0 copy-start.3
  0.0 68.8 %shard_map.46 = (bf16[4,2,16,1024]{3,2,1,0:T(8,128)(2,1)}, bf16[4,2,16,256]{3,2,1,0:T(8,128)(2,1)}) custom-call(bf16[32,61440]{1,0:T(8,128)(2,1)} %dens.1, bf16[1,15360,1024]{2,1,0:T(8,128)(2,1)} %basis.1), custom_call_target="tpu_custom_call" | custom-call | flops 4026531840 | bytes 35389440 | tf_op jit(solution)/shard_map/pallas_call | solution.py:414
  68.9 0.0 copy-done.2
  68.9 0.0 copy-done.3
  68.9 0.0 copy-start
  68.9 0.9 %copy-done = bf16[4,2,16,1024]{3,2,1,0:T(8,128)(2,1)S(1)} copy-done((bf16[4,2,16,1024]{3,2,1,0:T(8,128)(2,1)S(1)}, bf16[4,2,16,1024]{3,2,1,0:T(8,128)(2,1)}, u32[]{:S(2)}) %copy-start) | copy-done | bytes 262168
  69.8 0.0 copy-start.1
  69.8 0.8 %copy-done.1 = bf16[4,2,16,256]{3,2,1,0:T(8,128)(2,1)S(1)} copy-done((bf16[4,2,16,256]{3,2,1,0:T(8,128)(2,1)S(1)}, bf16[4,2,16,256]{3,2,1,0:T(8,128)(2,1)}, u32[]{:S(2)}) %copy-start.1) | copy-done | bytes 65560
  70.7 3.1 %shard_map.47 = f32[4,1024,256]{2,1,0:T(8,128)} custom-call(bf16[128,1024]{1,0:T(8,128)(2,1)S(1)} %bitcast.3, bf16[128,256]{1,0:T(8,128)(2,1)S(1)} %bitcast.4, f32[1,128]{1,0:T(1,128)S(1)} %bitcast.5, f32[4]{0:T(128)S(1)} %copy-done.3), custom_call_target="tpu_custom_call" | custom-call | tf_op jit(solution)/shard_map/pallas_call | solution.py:451
Async XLA Ops:
  0.0 68.9 %copy-start.2 = (f32[128]{0:T(128)S(1)}, f32[128]{0:T(128)}, u32[]{:S(2)}) copy-start(f32[128]{0:T(128)} %param.6) | copy-start | bytes 1540
  0.0 68.9 %copy-start.3 = (f32[4]{0:T(128)S(1)}, f32[4]{0:T(128)}, u32[]{:S(2)}) copy-start(f32[4]{0:T(128)} %frequencies.1) | copy-start | bytes 52
  68.9 1.0 %copy-start = (bf16[4,2,16,1024]{3,2,1,0:T(8,128)(2,1)S(1)}, bf16[4,2,16,1024]{3,2,1,0:T(8,128)(2,1)}, u32[]{:S(2)}) copy-start(bf16[4,2,16,1024]{3,2,1,0:T(8,128)(2,1)} %get-tuple-element.7) | copy-start | bytes 786436
  69.8 0.8 %copy-start.1 = (bf16[4,2,16,256]{3,2,1,0:T(8,128)(2,1)S(1)}, bf16[4,2,16,256]{3,2,1,0:T(8,128)(2,1)}, u32[]{:S(2)}) copy-start(bf16[4,2,16,256]{3,2,1,0:T(8,128)(2,1)} %get-tuple-element.8) | copy-start | bytes 196612

commit v4 on v3

--- a/solution.py
+++ b/solution.py
@@ -8,7 +8,9 @@
 from jax.sharding import PartitionSpec as P
 
 MESH = pl.DeviceIdType.MESH
-WIDTH = 1536
+WIDTH = 2560
+LAST_WIDTHS = (1536, 1024)
+RELAYED = (False, False)
 TILE = 256
 STAGES = 2
 AHEAD = 4
@@ -130,7 +132,7 @@
 
 
 def fused_kernel(
-    n, n_ga, chunks, dens, basis, coef_out, block_out, eig, exch, total, x_in, z_in, coef, other,
+    n, n_ga, widths, dens, basis, coef_out, block_out, eig, exch, total, x_in, z_in, coef, other,
     eig_sem, own_sem, send, recv, fwd_send, fwd_recv,
     x_send, x_recv, z_send, z_recv, all_send, all_recv, sib_send, sib_recv,
 ):
@@ -138,7 +140,8 @@
     depth, half = eig.shape
     _, stages, part, _ = coef.shape
     reach = depth // 2
-    width = reach // chunks
+    chunks = len(widths)
+    starts = [sum(widths[:k]) for k in range(chunks)]
     steps = stages * chunks
     groups = n * n_ga
     rank = z * n_ga + x
@@ -149,28 +152,28 @@
     crosses = (rank // n + c) % 2
 
     def eig_copy(k, h):
-        at = span(h * reach + k * width, width, 256)
+        at = span(h * reach + starts[k], widths[k], 128)
         return pltpu.make_async_copy(basis.at[0, at], eig.at[at], eig_sem.at[k, h])
 
     def own_copy():
-        return pltpu.make_async_copy(dens.at[:, span(z * depth, depth, 256)], exch.at[z], own_sem)
+        return pltpu.make_async_copy(dens.at[:, span(z * depth, depth, 128)], exch.at[z], own_sem)
 
     def piece(g):
         s, k = divmod(g, chunks)
-        return pl.ds(s * part, part), c * reach + k * width
+        return pl.ds(s * part, part), c * reach + starts[k], widths[k]
 
     def sending(g, d):
         to = flipped(z, d)
-        rows, at = piece(g)
-        return pltpu.make_async_remote_copy(
-            src_ref=dens.at[rows, span(to * depth + at, width, 256)],
-            dst_ref=exch.at[z, rows, span(at, width, 256)],
+        rows, at, width = piece(g)
+        return pltpu.make_async_remote_copy(
+            src_ref=dens.at[rows, span(to * depth + at, width, 128)],
+            dst_ref=exch.at[z, rows, span(at, width, 128)],
             send_sem=send.at[g, d - 1], recv_sem=recv.at[g, d - 1],
             device_id={"pair": to}, device_id_type=MESH)
 
     def forwarding(g, d):
-        rows, at = piece(g)
-        here = exch.at[flipped(z, d), rows, span(at, width, 256)]
+        rows, at, width = piece(g)
+        here = exch.at[flipped(z, d), rows, span(at, width, 128)]
         return pltpu.make_async_remote_copy(
             src_ref=here, dst_ref=here,
             send_sem=fwd_send.at[g, d - 1], recv_sem=fwd_recv.at[g, d - 1],
@@ -243,8 +246,32 @@
             acc = acc + z_in[s, d - 1]
         coef[kept(x), s, :, strip_of(z)] = acc.astype(jnp.bfloat16)
         for e in range(groups - 1, 0, -1):
-            sharing(s, e).start()
+            if not RELAYED[s] or e % n_ga == 0 or e < n_ga:
+                sharing(s, e).start()
         crossing(s).start()
+
+    def relaying(s, e):
+        d, e_x = divmod(e, n_ga)
+        here = coef.at[kept(x), s, :, strip_of(flipped(z, d))]
+        return pltpu.make_async_remote_copy(
+            src_ref=here, dst_ref=here,
+            send_sem=all_send.at[s, e - 1], recv_sem=all_recv.at[s, e - 1],
+            device_id={"ga": flipped(x, e_x)}, device_id_type=MESH)
+
+    def relay(s):
+        for d in far_first:
+            sharing(s, d * n_ga).wait_recv()
+            for e_x in range(1, n_ga):
+                relaying(s, d * n_ga + e_x).start()
+
+    def finish_sharing(s):
+        for e in range(1, groups):
+            if not RELAYED[s] or e < n_ga:
+                sharing(s, e).wait()
+            elif e % n_ga == 0:
+                sharing(s, e).wait_send()
+            else:
+                relaying(s, e).wait()
 
     def multiply(g):
         s, k = divmod(g, chunks)
@@ -258,7 +285,8 @@
             at = strip_of(j)
             acc = 0.0
             for h in range(2):
-                deep = pl.ds(h * reach + k * width, width)
+                width = widths[k]
+                deep = pl.ds(h * reach + starts[k], width)
                 left = exch[:, pl.ds(s * part, part), deep].reshape(n * part, width)
                 acc += jnp.dot(left, eig[deep, at], preferred_element_type=jnp.float32)
             acc = acc.reshape(n, part, strip)
@@ -309,6 +337,8 @@
         after.setdefault(done, []).append((begin_x, s))
         after.setdefault(done + gap, []).append((begin_z, s))
         after.setdefault(done + 2 * gap, []).append((begin_sharing, s))
+        if RELAYED[s]:
+            after.setdefault(done + 2 * gap + 1, []).append((relay, s))
 
     for g in range(steps + 1):
         if g < steps:
@@ -330,6 +360,8 @@
             sending(g, d).wait_send()
             forwarding(g, d).wait_send()
     begin_sharing(last)
+    if RELAYED[last]:
+        relay(last)
     for s in range(stages):
         for e in range(1, n_ga):
             for d in all_far_first:
@@ -337,8 +369,7 @@
         for d in far_first:
             z_sum(s, d).wait_send()
     for s in range(stages):
-        for e in range(1, groups):
-            sharing(s, e).wait()
+        finish_sharing(s)
 
     coef_out[...] = coef[...]
     for s in range(stages):
@@ -405,14 +436,15 @@
     rows = densities.shape[0]
     _, depth, half = eigvecs.shape
     groups = n * n_ga
-    chunks = depth // (2 * WIDTH)
+    widths = [WIDTH] * ((depth // 2 - sum(LAST_WIDTHS)) // WIDTH) + list(LAST_WIDTHS)
+    chunks = len(widths)
     part, block, share = rows // STAGES, 2 * half // groups, n // n_ga
     dma = pltpu.SemaphoreType.DMA
     any_space = pl.BlockSpec(memory_space=pl.ANY)
     vmem = pl.BlockSpec(memory_space=pltpu.VMEM)
     coef_shape, block_shape = (n, STAGES, part, half), (n, STAGES, part, block)
     coef, columns = pl.pallas_call(
-        functools.partial(fused_kernel, n, n_ga, chunks),
+        functools.partial(fused_kernel, n, n_ga, widths),
         out_shape=(
             jax.ShapeDtypeStruct(coef_shape, jnp.bfloat16),
             jax.ShapeDtypeStruct(block_shape, jnp.bfloat16),
@@ -465,7 +497,8 @@
     rows, depth, half = densities.shape[0], eigvecs.shape[1], eigvecs.shape[2]
     groups = n * n_ga
     fits = (
-        depth % (2 * WIDTH) == 0 and rows % (16 * STAGES) == 0 and n % n_ga == 0
+        depth % 256 == 0 and depth // 2 % WIDTH == sum(LAST_WIDTHS) % WIDTH
+        and depth // 2 > sum(LAST_WIDTHS) and rows % (16 * STAGES) == 0 and n % n_ga == 0
         and half % (128 * n) == 0 and n_ga == 2
     )
     if fits:

time: 74 us -> 75.4 us (1.019)
  Pallas kernels: 71.9 us -> 73.4 us
    pallas_call x1, Pallas kernels: 68.8 us -> 70.3 us  [fused(): pl.pallas_call(functools.partial(fused_kernel, n, n_ga, widths), out_shap...]
where the time goes in v4:
time: 75.4 us; the launch traced here: 75.2 us
  Pallas kernels  73.4 us (97%)
  local copies, waits for them, and re-layouts  1.79 us (2%)
    pallas_call x1, Pallas kernels, fused(): pl.pallas_call(functools.partial(fused_kernel, n, n_ga, widths), out_shap...  70.3 us
    pallas_call x1, Pallas kernels, final(): pl.pallas_call(functools.partial(final_kernel, -1.0 / pairs), out_shape=j...  3.11 us
    unnamed x8, local copies, waits for them, and re-layouts  1.79 us

profile of v4, /device:TPU:0, one launch (start us, length us, event | category | flops | bytes accessed | tf_op | source)
XLA Modules:
  0.0 75.2 jit_solution(8458320424219426759)
XLA Ops:
  0.0 0.0 copy-start.2
  0.0 0.0 copy-start.3
  0.0 70.3 %shard_map.46 = (bf16[4,2,16,1024]{3,2,1,0:T(8,128)(2,1)}, bf16[4,2,16,256]{3,2,1,0:T(8,128)(2,1)}) custom-call(bf16[32,61440]{1,0:T(8,128)(2,1)} %dens.1, bf16[1,15360,1024]{2,1,0:T(8,128)(2,1)} %basis.1), custom_call_target="tpu_custom_call" | custom-call | flops 4026531840 | bytes 35389440 | tf_op jit(solution)/shard_map/pallas_call | solution.py:446
  70.3 0.0 copy-done.2
  70.3 0.0 copy-done.3
  70.3 0.0 copy-start
  70.3 0.9 %copy-done = bf16[4,2,16,1024]{3,2,1,0:T(8,128)(2,1)S(1)} copy-done((bf16[4,2,16,1024]{3,2,1,0:T(8,128)(2,1)S(1)}, bf16[4,2,16,1024]{3,2,1,0:T(8,128)(2,1)}, u32[]{:S(2)}) %copy-start) | copy-done | bytes 262168
  71.3 0.0 copy-start.1
  71.3 0.8 %copy-done.1 = bf16[4,2,16,256]{3,2,1,0:T(8,128)(2,1)S(1)} copy-done((bf16[4,2,16,256]{3,2,1,0:T(8,128)(2,1)S(1)}, bf16[4,2,16,256]{3,2,1,0:T(8,128)(2,1)}, u32[]{:S(2)}) %copy-start.1) | copy-done | bytes 65560
  72.1 3.1 %shard_map.47 = f32[4,1024,256]{2,1,0:T(8,128)} custom-call(bf16[128,1024]{1,0:T(8,128)(2,1)S(1)} %bitcast.3, bf16[128,256]{1,0:T(8,128)(2,1)S(1)} %bitcast.4, f32[1,128]{1,0:T(1,128)S(1)} %bitcast.5, f32[4]{0:T(128)S(1)} %copy-done.3), custom_call_target="tpu_custom_call" | custom-call | tf_op jit(solution)/shard_map/pallas_call | solution.py:483
Async XLA Ops:
  0.0 70.3 %copy-start.2 = (f32[128]{0:T(128)S(1)}, f32[128]{0:T(128)}, u32[]{:S(2)}) copy-start(f32[128]{0:T(128)} %param.6) | copy-start | bytes 1540
  0.0 70.3 %copy-start.3 = (f32[4]{0:T(128)S(1)}, f32[4]{0:T(128)}, u32[]{:S(2)}) copy-start(f32[4]{0:T(128)} %frequencies.1) | copy-start | bytes 52
  70.3 1.0 %copy-start = (bf16[4,2,16,1024]{3,2,1,0:T(8,128)(2,1)S(1)}, bf16[4,2,16,1024]{3,2,1,0:T(8,128)(2,1)}, u32[]{:S(2)}) copy-start(bf16[4,2,16,1024]{3,2,1,0:T(8,128)(2,1)} %get-tuple-element.7) | copy-start | bytes 786436
  71.3 0.8 %copy-start.1 = (bf16[4,2,16,256]{3,2,1,0:T(8,128)(2,1)S(1)}, bf16[4,2,16,256]{3,2,1,0:T(8,128)(2,1)}, u32[]{:S(2)}) copy-start(bf16[4,2,16,256]{3,2,1,0:T(8,128)(2,1)} %get-tuple-element.8) | copy-start | bytes 196612
